TPU v7x, 32 devices: a whole 2x2x4 slice. The times are simulated.
32 devices in a mesh: lat: 8 (over z, y), lev: 4 (over x, core).
Axes of the slice: x: 2, y: 2, z: 4, core: 2. Of those that a mesh axis runs over, the one named last changes fastest.
Arguments:
- grid: bfloat16 [3, 1536, 32, 2816], P(None, 'lat', 'lev'), may hold values from -6 to 6
- legendre: bfloat16 [384, 769, 1280], P(('lat', 'lev')), may hold values from -6 to 6
- gauss_weights: float32 [1280], replicated, may hold values from 0.00078125 to 0.003125
- band_counts: int32 [8], replicated, may hold values from 1 to 192, 1280 in all
- pair_m: int32 [384], replicated, may hold values from 0 to 383, each once
- vert_modes: float32 [32, 32], replicated, may hold values from -1 to 1
- mode_depth: float32 [32], replicated, may hold values from 0.5 to 50
- diffusion: float32 [32], replicated, may hold values from 1 to 100
- pressure_balance_matrix: float32 [32, 32], replicated, may hold values from -1 to 1
Outputs:
- next_grid_rows: bfloat16 [3, 1536, 32, 2816], P(None, 'lat', 'lev')
Inputs may be any that keep to these rules, and one draw needn't show every extreme that they name: `band_counts`: latitudes in each band, in band order; the bands cover all 1280 latitudes and the fullest holds 192. `pair_m`: each of 0 to 383 once.
All inputs are finite; a program needn't handle non-finite values.
Results may differ from a plain program's by a relative error of at most 0.0072.
Values may be sent and summed in bfloat16 or wider, within the bound.
No kernel may reach another device: no remote copies, remote signals or barrier semaphores. Data moves between devices by JAX's collectives and lax.ppermute only.
A program may use at most 576 MiB of HBM per device.

v0:
```python
import functools
import math

import jax
import jax.numpy as jnp
from jax import lax
from jax.experimental import pallas as pl
from jax.experimental.pallas import tpu as pltpu
from jax.sharding import PartitionSpec as P

LANES = 128
VMEM_LIMIT = 63 * 1024 * 1024


def swap_units(parts, unit):
    lane = lax.broadcasted_iota(jnp.int32, parts[0].shape, 1)
    step = 1
    parts = list(parts)
    while step < len(parts):
        shift = unit * step
        high = (lane & shift) != 0
        for i in range(len(parts)):
            if not i & step:
                a, b = parts[i], parts[i | step]
                parts[i] = jnp.where(high, pltpu.roll(b, shift, 1), a)
                parts[i | step] = jnp.where(high, b, pltpu.roll(a, LANES - shift, 1))
        step *= 2
    return parts


def row_tile(rows, most):
    tile = most
    while rows % tile:
        tile -= 16
    return tile


def ordered_after(value, *others):
    anywhere = pl.BlockSpec(memory_space=pl.ANY)
    return pl.pallas_call(
        lambda *refs: None,
        in_specs=[anywhere] * (1 + len(others)),
        out_specs=anywhere,
        out_shape=jax.ShapeDtypeStruct(value.shape, value.dtype),
        input_output_aliases={0: 0},
        name="ordered_after",
    )(value, *others)


def unit_circle(wave, points):
    lane = lax.broadcasted_iota(jnp.int32, wave.shape, 1).astype(jnp.float32)
    product = wave.astype(jnp.float32) * lane
    rest = product - points * jnp.floor(product * (1.0 / points))
    quarter = jnp.floor(rest * (4.0 / points) + 0.5)
    x = (rest - quarter * (points / 4.0)) * (2.0 * math.pi / points)
    y = x * x
    sine = x * (1 + y * (-1 / 6 + y * (1 / 120 + y * (-1 / 5040 + y * (1 / 362880)))))
    cosine = 1 + y * (-1 / 2 + y * (1 / 24 + y * (-1 / 720 + y * (1 / 40320))))
    odd = jnp.logical_or(quarter == 1, quarter == 3)
    cos_low = jnp.logical_or(quarter == 1, quarter == 2)
    sin_low = jnp.logical_or(quarter == 2, quarter == 3)
    cos_all = jnp.where(odd, sine, cosine)
    sin_all = jnp.where(odd, cosine, sine)
    return jnp.where(cos_low, -cos_all, cos_all), jnp.where(sin_low, -sin_all, sin_all)


def wave_rows(pair_ref, pair_dev, group, width, pair_group, device, parity):
    row = lax.broadcasted_iota(jnp.int32, (2 * group, LANES), 0)
    wave = jnp.full((2 * group, LANES), -1, jnp.int32)
    for b in range(group):
        pair = pair_group * group + b
        lower = pair_ref[device * pair_dev + jnp.minimum(pair, pair_dev - 1)]
        chosen = jnp.where(lower % 2 == parity, lower, width - 1 - lower)
        wave = jnp.where(jnp.logical_and(row % group == b, pair < pair_dev), chosen, wave)
    return wave


def fill_table(table, pair_ref, pair_dev, group, width, points, pair_group, first_device):
    unit = 2 * group
    count = 8 * unit

    @pl.loop(0, table.shape[1] // count)
    def _(n):
        at = pl.ds(pl.multiple_of(n * count, count), count)
        for parity in range(2):
            wave = jnp.concatenate(
                [
                    wave_rows(
                        pair_ref,
                        pair_dev,
                        group,
                        width,
                        pair_group,
                        first_device + n // 2 * 16 + n % 2 * 4 + j % 2 * 8 + j // 2,
                        parity,
                    )
                    for j in range(8)
                ],
                axis=0,
            )
            cos, sin = unit_circle(wave, points)
            cos, sin = jnp.where(wave < 0, 0.0, cos), jnp.where(wave < 0, 0.0, sin)
            half = LANES // 2
            cos_half, sin_half = cos[:, half : half + 1], sin[:, half : half + 1]
            cos_turn = jnp.broadcast_to(cos_half * cos_half - sin_half * sin_half, cos.shape)
            sin_turn = jnp.broadcast_to(2.0 * sin_half * cos_half, cos.shape)
            sine = lax.broadcasted_iota(jnp.int32, cos.shape, 0) // group % 2 == 1
            value, other = jnp.where(sine, -sin, cos), jnp.where(sine, cos, sin)
            for a in range(table.shape[2] // LANES):
                table[parity, at, a * LANES : (a + 1) * LANES] = value.astype(table.dtype)
                value, other = (
                    value * cos_turn - other * sin_turn,
                    other * cos_turn + value * sin_turn,
                )


def table_kernel(pair_dev, group, width, points, wide, pair_ref, table):
    fill_table(
        table, pair_ref, pair_dev, group, width, points, pl.program_id(0), pl.program_id(1) * wide
    )


def devices_at_once(devices):
    return 32 if devices % 32 == 0 else 16


def trig_table(pair_m, width, points, devices, groups, group):
    wide = devices_at_once(devices)
    rows = wide * 2 * group
    steps = devices // wide
    return pl.pallas_call(
        functools.partial(table_kernel, pair_m.shape[0] // devices, group, width, points, wide),
        grid_spec=pltpu.PrefetchScalarGridSpec(
            num_scalar_prefetch=1,
            grid=(groups, steps),
            in_specs=[],
            out_specs=pl.BlockSpec((2, rows, points // 2), lambda i, t, m: (0, i * steps + t, 0)),
        ),
        out_shape=jax.ShapeDtypeStruct((2, groups * steps * rows, points // 2), jnp.bfloat16),
        cost_estimate=pl.CostEstimate(
            flops=8 * groups * steps * rows * points,
            bytes_accessed=2 * groups * steps * rows * points,
            transcendentals=0,
        ),
        name="trig_table",
    )(pair_m)


def fold(lines):
    half = lines.shape[1] // 2
    low, high = lines[:, :half], lines[:, half:]
    return low + high, low - high


def emit_blocks(folded, table, scratch, store, tile, levels, unit):
    for parity in range(2):
        values = lax.dot_general(
            folded[parity], table[parity], (((1,), (1,)), ((), ())),
            preferred_element_type=jnp.float32,
        )
        for n in range(values.shape[1] // LANES):
            scratch[parity, n] = values[:, n * LANES : (n + 1) * LANES]
    for n in range(scratch.shape[1]):
        by_level = [
            swap_units(
                [
                    scratch[parity, n, pl.ds(l, tile, stride=levels), :].astype(jnp.bfloat16)
                    for parity in range(2)
                ],
                unit // 2,
            )
            for l in range(levels)
        ]
        for b in range(2):
            for a, part in enumerate(swap_units([x[b] for x in by_level], unit)):
                store(n * 2 * levels + b * levels + a, part)


def forward_kernel(levels, unit, some, grid_ref, table_ref, out_ref, folded, scratch):
    cap = grid_ref.shape[1] // levels
    tile = row_tile(cap, 32)

    @pl.when(jnp.logical_and(pl.program_id(0) % some == 0, pl.program_id(1) == 0))
    def _():
        for s in range(0, cap, tile):
            lines = slice(s * levels, (s + tile) * levels)
            folded[0, lines, :], folded[1, lines, :] = fold(grid_ref[0, lines, :])

    tables = [table_ref[0], table_ref[1]]
    for s in range(0, cap, tile):
        lines = slice(s * levels, (s + tile) * levels)

        def store(d, block, s=s):
            out_ref[d, 0, s : s + tile, :] = block

        emit_blocks(
            [folded[0, lines, :], folded[1, lines, :]],
            tables,
            scratch.at[s // tile],
            store,
            tile,
            levels,
            unit,
        )


def forward(fields, groups, grid, table, levels, unit, devices):
    _, rows, points = grid.shape
    cap = rows // levels
    tile = row_tile(cap, 32)
    wide = devices_at_once(devices)
    steps = devices // wide
    (first_field, some_fields), (first, some) = fields, groups
    count = some_fields * some
    columns = count * devices * unit
    half = wide * unit // 2
    return pl.pallas_call(
        functools.partial(forward_kernel, levels, unit, some),
        grid=(count, steps),
        in_specs=[
            pl.BlockSpec((1, rows, points), lambda i, t: (first_field + i // some, 0, 0)),
            pl.BlockSpec(
                (2, half, points // 2), lambda i, t: (0, (first + i % some) * steps + t, 0)
            ),
        ],
        out_specs=pl.BlockSpec((wide, 1, cap, LANES), lambda i, t: (t, i, 0, 0)),
        out_shape=jax.ShapeDtypeStruct((devices, count, cap, LANES), jnp.bfloat16),
        scratch_shapes=[
            pltpu.VMEM((2, rows, points // 2), jnp.bfloat16),
            pltpu.VMEM((cap // tile, 2, half // LANES, tile * levels, LANES), jnp.float32),
        ],
        compiler_params=pltpu.CompilerParams(vmem_limit_bytes=VMEM_LIMIT),
        cost_estimate=pl.CostEstimate(
            flops=rows * points * columns,
            bytes_accessed=2 * (some_fields * rows * points + rows * columns),
            transcendentals=0,
        ),
        name="forward_dft",
    )(grid, table)


def first_kernel(levels, unit, pair_dev, group, width, pair_ref, grid_ref, out_ref, table, scratch):
    @pl.when(pl.program_id(0) == 0)
    def _():
        fill_table(table, pair_ref, pair_dev, group, width, grid_ref.shape[2], 0, 0)

    tile = grid_ref.shape[1] // levels
    half = scratch.shape[2] * LANES
    folded = fold(grid_ref[0])
    for n in range(table.shape[1] // half):

        def store(d, block, n=n):
            out_ref[n * 2 * half // unit + d, 0] = block

        rows = slice(n * half, (n + 1) * half)
        emit_blocks(
            folded,
            [table[0, rows, :], table[1, rows, :]],
            scratch.at[n],
            store,
            tile,
            levels,
            unit,
        )


def forward_first(grid, pair_m, levels, unit, devices, group, width):
    _, rows, points = grid.shape
    cap = rows // levels
    tile = row_tile(cap, 32)
    columns = devices * unit
    half = devices_at_once(devices) * unit // 2
    return pl.pallas_call(
        functools.partial(first_kernel, levels, unit, pair_m.shape[0] // devices, group, width),
        grid_spec=pltpu.PrefetchScalarGridSpec(
            num_scalar_prefetch=1,
            grid=(cap // tile,),
            in_specs=[pl.BlockSpec((1, tile * levels, points), lambda t, m: (0, t, 0))],
            out_specs=pl.BlockSpec((devices, 1, tile, LANES), lambda t, m: (0, 0, t, 0)),
            scratch_shapes=[
                pltpu.VMEM((2, columns // 2, points // 2), jnp.bfloat16),
                pltpu.VMEM(
                    (columns // 2 // half, 2, half // LANES, tile * levels, LANES), jnp.float32
                ),
            ],
        ),
        out_shape=jax.ShapeDtypeStruct((devices, 1, cap, LANES), jnp.bfloat16),
        compiler_params=pltpu.CompilerParams(vmem_limit_bytes=VMEM_LIMIT),
        cost_estimate=pl.CostEstimate(
            flops=rows * points * columns,
            bytes_accessed=2 * rows * (points + columns),
            transcendentals=0,
        ),
        name="forward_first",
    )(pair_m, grid)


def inverse_kernel(levels, unit, groups, first_row, count_ref, *refs):
    spec_refs, table_ref = refs[:groups], refs[groups]
    out_ref, token_ref, turned = refs[-3:]
    devices, rows, _ = spec_refs[0].shape
    tile = row_tile(rows, 32)
    blocks = [(i, d) for i in range(groups) for d in range(0, devices, 2 * levels)]
    base = first_row + pl.program_id(0) * rows
    half = out_ref.shape[2] // 2
    for s in range(0, rows, tile):
        lines = pl.ds(s * levels, tile * levels)
        for n, (i, d) in enumerate(blocks):
            by_level = [
                swap_units(
                    [
                        spec_refs[i][d + b * levels + a, s : s + tile, :]
                        for a in range(levels)
                    ],
                    unit,
                )
                for b in range(2)
            ]
            for l in range(levels):
                parts = swap_units([by_level[0][l], by_level[1][l]], unit // 2)
                for parity in range(2):
                    turned[parity, n, pl.ds(s * levels + l, tile, stride=levels), :] = parts[
                        parity
                    ].astype(jnp.float32)
        row = lax.broadcasted_iota(jnp.int32, (tile * levels, LANES), 0)
        valid = row < (count_ref[0] - base - s) * levels
        even, odd = [
            jnp.dot(
                jnp.concatenate(
                    [
                        jnp.where(valid, turned[parity, n, lines, :], 0.0).astype(jnp.bfloat16)
                        for n in range(len(blocks))
                    ],
                    axis=1,
                ),
                table_ref[parity],
                preferred_element_type=jnp.float32,
            )
            for parity in range(2)
        ]
        out_ref[0, lines, :half] = (even + odd).astype(out_ref.dtype)
        out_ref[0, lines, half:] = (even - odd).astype(out_ref.dtype)
    token_ref[...] = jnp.zeros_like(token_ref)


def inverse(field, first_row, size, spec, offset, groups, table, count, partial, shape, levels, unit):
    devices = spec.shape[0]
    columns, points = 2 * table.shape[1], 2 * table.shape[2]
    tile = row_tile(size, 64 if size % 64 == 0 and offset % 64 == 0 else 32)
    if size <= 64:
        tile = row_tile(size, 32)
    rows = tile * levels

    def part(i):
        return pl.BlockSpec(
            (devices, tile, LANES), lambda t, c: (0, (offset + i * size) // tile + t, 0)
        )

    in_specs = [part(i) for i in range(groups)]
    in_specs.append(pl.BlockSpec(table.shape, lambda t, c: (0, 0, 0)))
    operands = [spec] * groups + [table]
    if partial is not None:
        in_specs.append(pl.BlockSpec(memory_space=pl.ANY))
        operands.append(partial)
    return pl.pallas_call(
        functools.partial(inverse_kernel, levels, unit, groups, first_row),
        grid_spec=pltpu.PrefetchScalarGridSpec(
            num_scalar_prefetch=1,
            grid=(size // tile,),
            in_specs=in_specs,
            out_specs=[
                pl.BlockSpec((1, rows, points), lambda t, c: (field, first_row // tile + t, 0)),
                pl.BlockSpec((8, LANES), lambda t, c: (0, 0)),
            ],
            scratch_shapes=[pltpu.VMEM((2, columns // 2 // LANES, rows, LANES), jnp.float32)],
        ),
        out_shape=[
            jax.ShapeDtypeStruct(shape, jnp.bfloat16),
            jax.ShapeDtypeStruct((8, LANES), jnp.float32),
        ],
        input_output_aliases={} if partial is None else {groups + 2: 0},
        compiler_params=pltpu.CompilerParams(vmem_limit_bytes=VMEM_LIMIT),
        cost_estimate=pl.CostEstimate(
            flops=size * levels * points * columns,
            bytes_accessed=2 * size * levels * (points + columns) + columns * points,
            transcendentals=0,
        ),
        name="inverse_dft",
    )(count, *operands)


def lane_levels(levels, group):
    lane = lax.broadcasted_iota(jnp.int32, (LANES, levels * group), 0)
    level = lax.broadcasted_iota(jnp.int32, (LANES, levels * group), 1)
    held = lane % group * levels + lane // (4 * group)
    return (held == level).astype(jnp.float32)


def exact_dot(a, b, dims=((1,), (0,))):
    return lax.dot_general(
        a, b, (dims, ((), ())), precision=lax.Precision.HIGHEST, preferred_element_type=jnp.float32
    )


def lane_matrix(matrix, levels, group):
    chosen = lane_levels(levels, group)
    spread = exact_dot(exact_dot(chosen, matrix), chosen, ((1,), (1,)))
    row = lax.broadcasted_iota(jnp.int32, spread.shape, 0)
    lane = lax.broadcasted_iota(jnp.int32, spread.shape, 1)
    return jnp.where(row // group % 4 == lane // group % 4, spread, 0.0)


def legendre_kernel(
    kind, first, pair_dev, lat_groups, group, outs, counts_ref, waves_ref, recv_ref, leg_ref, *rest
):
    weight_ref, rest = rest[0], rest[1:]
    gathered, made = rest[-2:]
    rest, out_refs = rest[:-2], rest[-2 - outs : -2]
    level_ref = rest[0]
    if kind == "divergence":
        modes_ref, div_out = rest[1], out_refs[-1]
        out_refs = out_refs[:-1]
    if kind == "temperature":
        balance_ref, div_in = rest[1:3]
    levels = level_ref.shape[1] // group
    row_count, lat_total = leg_ref.shape[1:]
    width = row_count - 1
    cap = recv_ref.shape[2]
    member = pl.program_id(1)
    pair = (first + pl.program_id(0)) * group + member

    @pl.when(member == 0)
    def _():
        start = 0
        for g in range(lat_groups):
            parts = [recv_ref[g * group + h, 0] for h in range(group)]
            for b, part in enumerate(swap_units(parts, 1)):
                gathered[b, pl.ds(start, cap), :] = part.astype(jnp.float32)
            start = start + counts_ref[g]

    @pl.when(pair < pair_dev)
    def _():
        wave = waves_ref[pair]
        coeffs = (gathered[member, :lat_total, :] * weight_ref[...]).astype(jnp.bfloat16)
        main = leg_ref[0, :width, :]
        last = jnp.broadcast_to(leg_ref[0, width:, :], (16, lat_total))
        spectral = jnp.concatenate(
            [
                jnp.dot(main, coeffs, preferred_element_type=jnp.float32),
                jnp.dot(last, coeffs, preferred_element_type=jnp.float32),
            ],
            axis=0,
        )
        shape = spectral.shape
        row = lax.broadcasted_iota(jnp.int32, shape, 0)
        lane = lax.broadcasted_iota(jnp.int32, shape, 1)
        own = row < width - wave
        upper = lane // (2 * group) % 2 != wave % 2
        keep = jnp.logical_and(jnp.logical_xor(own, upper), row < row_count)
        degree = jnp.where(own, row + wave, row - 1)
        ratio = (degree * (degree + 1)).astype(jnp.float32) / float(width * (width - 1))
        spectral = jnp.where(keep, spectral, 0.0)
        if kind != "temperature":
            per_level = jnp.broadcast_to(level_ref[...], (8, level_ref.shape[1]))
            per_lane = exact_dot(per_level, lane_levels(levels, group), ((1,), (1,)))[:1]
        if kind == "vorticity":
            new = spectral / (1.0 + per_lane * ratio * ratio)
        elif kind == "divergence":
            modes_matrix = lane_matrix(modes_ref[...], levels, group)
            modes = exact_dot(spectral, modes_matrix, ((1,), (1,)))
            modes = modes / (1.0 + per_lane * ratio)
            new = exact_dot(modes, modes_matrix)
            div_out[0] = new
        else:
            balance = lane_matrix(balance_ref[...], levels, group)
            new = spectral - exact_dot(div_in[0], balance, ((1,), (1,)))
        zonal = jnp.logical_and(wave == 0, jnp.logical_not(upper))
        new = new * jnp.where(zonal, 1.0, 2.0)
        tail = jnp.concatenate(
            [new[width:], jnp.zeros((LANES - 16, LANES), jnp.float32)], axis=0
        )
        turned = jnp.dot(
            new[:width].T.astype(jnp.bfloat16), main, preferred_element_type=jnp.float32
        )
        turned += jnp.dot(
            tail.T.astype(jnp.bfloat16),
            jnp.broadcast_to(leg_ref[0, width:, :], (LANES, lat_total)),
            preferred_element_type=jnp.float32,
        )
        made[member, :lat_total, :] = turned.T
        made[member, lat_total:, :] = jnp.zeros((cap, LANES), jnp.float32)

    @pl.when(pair >= pair_dev)
    def _():
        made[member] = jnp.zeros(made.shape[1:], jnp.float32)

    @pl.when(member == group - 1)
    def _():
        start = 0
        for g in range(lat_groups):
            parts = [made[b, pl.ds(start, cap), :].astype(jnp.bfloat16) for b in range(group)]
            for h, part in enumerate(swap_units(parts, 1)):
                row = 0
                for out_ref in out_refs:
                    size = out_ref.shape[1]
                    out_ref[g * group + h] = part[row : row + size]
                    row += size
            start = start + counts_ref[g]


def legendre_step(
    kind, first, some, source, received, targets, legendre, weights, counts, waves, levels, extra, group, partial
):
    devices, _, cap, _ = received.shape
    pair_dev, row_count, lat_total = legendre.shape
    lat_groups = devices // group

    def at_pair(i, b, *_):
        return (jnp.minimum((first + i) * group + b, pair_dev - 1), 0, 0)

    def whole(i, b, *_):
        return (0, 0)

    def blocks(size, offset):
        return pl.BlockSpec(
            (devices, size, LANES), lambda i, b, *_: (0, offset // size + first + i, 0)
        )

    square = pl.BlockSpec(extra[0].shape, whole) if extra else None
    div_block = pl.BlockSpec((1, row_count + 15, LANES), at_pair)
    in_specs = [
        pl.BlockSpec((devices, 1, cap, LANES), lambda i, b, *_: (0, source + i, 0, 0)),
        pl.BlockSpec((1, row_count, lat_total), at_pair),
        pl.BlockSpec((lat_total, LANES), whole),
        pl.BlockSpec((1, levels.shape[0]), whole),
    ]
    out_specs = [blocks(size, offset) for size, offset, _ in targets]
    out_shape = [
        jax.ShapeDtypeStruct((devices, total, LANES), jnp.bfloat16) for _, _, total in targets
    ]
    if kind == "divergence":
        in_specs.append(square)
        out_specs.append(div_block)
        out_shape.append(jax.ShapeDtypeStruct((pair_dev, row_count + 15, LANES), jnp.float32))
    elif kind == "temperature":
        in_specs += [square, div_block]
    operands = [counts, waves, received, legendre, weights, levels[None, :], *extra]
    aliases = {}
    if partial is not None:
        aliases = {len(operands): 0}
        in_specs.append(pl.BlockSpec(memory_space=pl.ANY))
        operands.append(partial)
    held = pltpu.VMEM((group, lat_total + cap, LANES), jnp.float32)
    return pl.pallas_call(
        functools.partial(
            legendre_kernel, kind, first, pair_dev, lat_groups, group, len(out_specs)
        ),
        grid_spec=pltpu.PrefetchScalarGridSpec(
            num_scalar_prefetch=2,
            grid=(some, group),
            in_specs=in_specs,
            out_specs=out_specs,
            scratch_shapes=[held, held],
        ),
        out_shape=out_shape,
        input_output_aliases=aliases,
        compiler_params=pltpu.CompilerParams(vmem_limit_bytes=VMEM_LIMIT),
        cost_estimate=pl.CostEstimate(
            flops=8 * some * group * row_count * lat_total * LANES,
            bytes_accessed=2 * some * (group * row_count * lat_total + 2 * devices * cap * LANES),
            transcendentals=0,
        ),
        name="legendre_" + kind,
    )(*operands)


def shards(
    grid,
    legendre,
    gauss_weights,
    band_counts,
    pair_m,
    vert_modes,
    mode_depth,
    diffusion,
    pressure_balance_matrix,
):
    lat_groups = lax.axis_size("lat")
    group = lax.axis_size("lev")
    devices = lat_groups * group
    fields, cap, levels, points = grid.shape
    pair_dev, row_count, _ = legendre.shape
    width = row_count - 1
    unit = 4 * group
    groups = -(-pair_dev // group)
    band = lax.axis_index("lat")
    owner = band * group + lax.axis_index("lev")


    bands = jnp.arange(lat_groups, dtype=jnp.int32)
    count = jnp.sum(jnp.where(bands == band, band_counts, 0))
    weights = jnp.broadcast_to((gauss_weights / points)[:, None], (gauss_weights.shape[0], LANES))
    waves = lax.dynamic_slice(pair_m, (owner * pair_dev,), (pair_dev,))

    rows = grid.reshape(fields, cap * levels, points)

    def exchange(blocks):
        return lax.all_to_all(
            blocks, ("lat", "lev"), split_axis=0, concat_axis=0, tiled=True
        )

    sent = forward_first(rows, pair_m, levels, unit, devices, group, width)
    received = [(0, 1, exchange(sent))]
    later_m, _ = lax.optimization_barrier((pair_m, sent))
    table = trig_table(later_m, width, points, devices, groups, group)
    dft = functools.partial(
        forward, grid=rows, table=table, levels=levels, unit=unit, devices=devices
    )
    if groups > 1:
        sent = dft((0, 1), (1, groups - 1))
        received.append((1, groups - 1, exchange(sent)))
    others = exchange(dft((1, fields - 1), (0, groups)))

    step = functools.partial(
        legendre_step,
        legendre=legendre,
        weights=weights,
        counts=band_counts,
        waves=waves,
        group=group,
    )
    vorticity = None
    for first, some, blocks in received:
        (vorticity,) = step(
            "vorticity",
            first,
            some,
            0,
            blocks,
            targets=[(cap, 0, groups * cap)],
            levels=diffusion,
            extra=(),
            partial=vorticity,
        )
    vorticity = exchange(ordered_after(vorticity, others))
    late = max(16, cap // 3 // 16 * 16)
    if late >= cap or groups * (cap - late) % cap or (cap - late) % late:
        late = 0
    main, offset = cap - late, groups * (cap - late)
    total = offset + groups * cap
    back, new_divergence = step(
        "divergence",
        0,
        groups,
        0,
        others,
        targets=[(cap, offset, total)],
        levels=mode_depth,
        extra=(vert_modes,),
        partial=None,
    )
    targets = [(main, 0, total)] + ([(late, 0, groups * late)] if late else [])
    back, *rest = step(
        "temperature",
        0,
        groups,
        groups,
        others,
        targets=targets,
        levels=diffusion,
        extra=(pressure_balance_matrix, new_divergence),
        partial=back,
    )
    to_grid = functools.partial(
        inverse,
        groups=groups,
        table=table,
        count=count[None],
        shape=(fields, cap * levels, points),
        levels=levels,
        unit=unit,
    )
    out, token = to_grid(0, 0, cap, vorticity, 0, partial=None)
    back = exchange(back)
    if late:
        last = exchange(ordered_after(rest[0], back, token))
    out, _ = to_grid(1, 0, cap, back, offset, partial=out)
    out, _ = to_grid(2, 0, main, back, 0, partial=out)
    if late:
        out, _ = to_grid(2, main, late, last, 0, partial=out)
    return out.reshape(fields, cap, levels, points)


def solution(mesh):
    placed = (
        P(None, "lat", "lev", None),
        P(("lat", "lev"), None, None),
        P(),
        P(),
        P(),
        P(),
        P(),
        P(),
        P(),
    )
    return jax.shard_map(
        shards, mesh=mesh, in_specs=placed, out_specs=P(None, "lat", "lev", None), check_vma=False
    )
```

profile of v0, /device:TPU:0, one launch (start us, length us, event | category | flops | bytes accessed | tf_op | source)
XLA Modules:
  0.0 683.7 jit_solution(11171458309733293015)
XLA Ops:
  0.0 11.7 %forward_first.1 = bf16[32,1,192,128]{3,2,1,0:T(8,128)(2,1)} custom-call(s32[384]{0:T(512)} %pair_ref.2, bf16[3,1536,2816]{2,1,0:T(8,128)(2,1)} %bitcast.5), custom_call_target="tpu_custom_call" | custom-call | flops 2214592512 | bytes 10223616 | tf_op jit(solution)/shard_map/forward_first/pallas_call | solution.py:273
  11.7 7.4 %all-to-all-start.3 = ((bf16[32,1,192,128]{3,2,1,0:T(8,128)(2,1)}), bf16[32,1,192,128]{3,2,1,0:T(8,128)(2,1)}, u32[]{:S(2)}, u32[]{:S(2)}) async-start(bf16[32,1,192,128]{3,2,1,0:T(8,128)(2,1)} %forward_first.1), calls=%async_computation.3 | async-start | bytes 3145728 | tf_op jit(solution)/shard_map/all_to_all | solution.py:608
  19.1 6.9 %trig_table.1.table_ref.refs_3_ = bf16[2,768,1408]{2,1,0:T(8,128)(2,1)} custom-call(s32[384]{0:T(512)} %pair_ref.2), custom_call_target="tpu_custom_call" | custom-call | flops 17301504 | bytes 4325376 | tf_op jit(solution)/shard_map/trig_table/pallas_call | solution.py:131
  26.0 12.4 %forward_dft.3 = bf16[32,2,192,128]{3,2,1,0:T(8,128)(2,1)} custom-call(bf16[3,1536,2816]{2,1,0:T(8,128)(2,1)} %bitcast.6, bf16[2,768,1408]{2,1,0:T(8,128)(2,1)} %trig_table.1.table_ref.refs_3_), custom_call_target="tpu_custom_call" | custom-call | flops 4429185024 | bytes 11796480 | tf_op jit(solution)/shard_map/forward_dft/pallas_call | solution.py:217
  38.5 18.3 %all-to-all-done.3.recv_ref = bf16[32,1,192,128]{3,2,1,0:T(8,128)(2,1)} async-done(((bf16[32,1,192,128]{3,2,1,0:T(8,128)(2,1)}), bf16[32,1,192,128]{3,2,1,0:T(8,128)(2,1)}, u32[]{:S(2)}, u32[]{:S(2)}) %all-to-all-start.3) | async-done | bytes 1572896 | tf_op jit(solution)/shard_map/all_to_all | solution.py:608
  56.8 3.9 all-to-all-start.2
  60.7 28.1 %forward_dft.2 = bf16[32,6,192,128]{3,2,1,0:T(8,128)(2,1)} custom-call(bf16[3,1536,2816]{2,1,0:T(8,128)(2,1)} %bitcast.7, bf16[2,768,1408]{2,1,0:T(8,128)(2,1)} %trig_table.1.table_ref.refs_3_), custom_call_target="tpu_custom_call" | custom-call | flops 13287555072 | bytes 26738688 | tf_op jit(solution)/shard_map/forward_dft/pallas_call | solution.py:217
  88.8 43.4 %all-to-all-done.2.recv_ref = bf16[32,2,192,128]{3,2,1,0:T(8,128)(2,1)} async-done(((bf16[32,2,192,128]{3,2,1,0:T(8,128)(2,1)}), bf16[32,2,192,128]{3,2,1,0:T(8,128)(2,1)}, u32[]{:S(2)}, u32[]{:S(2)}) %all-to-all-start.2) | async-done | bytes 3145760 | tf_op jit(solution)/shard_map/all_to_all | solution.py:608
  132.2 4.2 all-to-all-start
  138.9 14.0 %legendre_vorticity.2.rest_2_ = bf16[32,576,128]{2,1,0:T(8,128)(2,1)} custom-call(s32[8]{0:T(128)} %counts_ref.7, s32[12]{0:T(128)} %dynamic_slice.3.waves_ref, bf16[32,1,192,128]{3,2,1,0:T(8,128)(2,1)} %all-to-all-done.3.recv_ref, bf16[12,769,1280]{2,1,0:T(8,128)(2,1)} %leg_ref.7, f32[1280,128]{1,0:T(8,128)} %broadcast_in_dim.23.rest_0_, f32[1,32]{1,0:T(1,128)} %bitcast.8), custom_call_target="tpu_custom_call" | custom-call | flops 4031774720 | bytes 11020288 | tf_op jit(solution)/shard_map/legendre_vorticity/pallas_call | solution.py:554
  152.9 24.2 %legendre_vorticity.3.refs_0_ = bf16[32,576,128]{2,1,0:T(8,128)(2,1)} custom-call(s32[8]{0:T(128)} %counts_ref.7, s32[12]{0:T(128)} %dynamic_slice.3.waves_ref, bf16[32,2,192,128]{3,2,1,0:T(8,128)(2,1)} %all-to-all-done.2.recv_ref, bf16[12,769,1280]{2,1,0:T(8,128)(2,1)} %leg_ref.7, ...), custom_call_target="tpu_custom_call", output_to_operand_aliasing={{}: (6, {})} | custom-call | flops 8063549440 | bytes 22040576 | tf_op jit(solution)/shard_map/legendre_vorticity/pallas_call | solution.py:554
  177.0 168.5 %all-to-all-done.recv_ref.refs_1_ = bf16[32,6,192,128]{3,2,1,0:T(8,128)(2,1)} async-done(((bf16[32,6,192,128]{3,2,1,0:T(8,128)(2,1)}), bf16[32,6,192,128]{3,2,1,0:T(8,128)(2,1)}, u32[]{:S(2)}, u32[]{:S(2)}) %all-to-all-start) | async-done | bytes 9437216 | tf_op jit(solution)/shard_map/all_to_all | solution.py:608
  345.5 3.8 all-to-all-start.4
  349.3 52.2 %legendre_divergence.1 = (bf16[32,960,128]{2,1,0:T(8,128)(2,1)}, f32[12,784,128]{2,1,0:T(8,128)}) custom-call(s32[8]{0:T(128)} %counts_ref.7, s32[12]{0:T(128)} %dynamic_slice.3.waves_ref, bf16[32,6,192,128]{3,2,1,0:T(8,128)(2,1)} %all-to-all-done.recv_ref.refs_1_, bf16[12,769,1280]{2,1,0:T(8,128)(2,1)} %leg_ref.7, f32[1280,128]{1,0:T(8,128)} %broadcast_in_dim.23.rest_0_, ...), custom_call_target="tpu_custom_call" | custom-call | flops 12095324160 | bytes 33060864 | tf_op jit(solution)/shard_map/legendre_divergence/pallas_call | solution.py:554
  401.5 36.7 %legendre_temperature.1 = (bf16[32,960,128]{2,1,0:T(8,128)(2,1)}, bf16[32,192,128]{2,1,0:T(8,128)(2,1)}) custom-call(s32[8]{0:T(128)} %counts_ref.7, s32[12]{0:T(128)} %dynamic_slice.3.waves_ref, bf16[32,6,192,128]{3,2,1,0:T(8,128)(2,1)} %all-to-all-done.recv_ref.refs_1_, bf16[12,769,1280]{2,1,0:T(8,128)(2,1)} %leg_ref.7, ...), custom_call_target="tpu_custom_call", output_to_operand_aliasing={{0}: (8, {})} | custom-call | flops 12095324160 | bytes 33060864 | tf_op jit(solution)/shard_map/legendre_temperature/pallas_call | solution.py:554
  438.2 16.4 %all-to-all-done.4.refs_0_.refs_1_.refs_2_ = bf16[32,576,128]{2,1,0:T(8,128)(2,1)} async-done(((bf16[32,576,128]{2,1,0:T(8,128)(2,1)}), bf16[32,576,128]{2,1,0:T(8,128)(2,1)}, u32[]{:S(2)}, u32[]{:S(2)}) %all-to-all-start.4) | async-done | bytes 4718624 | tf_op jit(solution)/shard_map/all_to_all | solution.py:608
  454.7 3.8 all-to-all-start.1
  459.1 16.1 %inverse_dft.4 = (bf16[3,1536,2816]{2,1,0:T(8,128)(2,1)}, f32[8,128]{1,0:T(8,128)}) custom-call(s32[1]{0:T(128)} %bitcast.count_ref, bf16[32,576,128]{2,1,0:T(8,128)(2,1)} %all-to-all-done.4.refs_0_.refs_1_.refs_2_, bf16[32,576,128]{2,1,0:T(8,128)(2,1)} %all-to-all-done.4.refs_0_.refs_1_.refs_2_, ...), custom_call_target="tpu_custom_call" | custom-call | flops 6643777536 | bytes 17694720 | tf_op jit(solution)/shard_map/inverse_dft/pallas_call | solution.py:365
  475.2 157.8 %all-to-all-done.1.refs_1_.refs_0_.refs_2_ = bf16[32,960,128]{2,1,0:T(8,128)(2,1)} async-done(((bf16[32,960,128]{2,1,0:T(8,128)(2,1)}), bf16[32,960,128]{2,1,0:T(8,128)(2,1)}, u32[]{:S(2)}, u32[]{:S(2)}) %all-to-all-start.1) | async-done | bytes 7864352 | tf_op jit(solution)/shard_map/all_to_all | solution.py:608
  633.1 3.7 all-to-all-start.5
  636.7 16.1 %inverse_dft.5 = (bf16[3,1536,2816]{2,1,0:T(8,128)(2,1)}, f32[8,128]{1,0:T(8,128)}) custom-call(s32[1]{0:T(128)} %bitcast.count_ref, bf16[32,960,128]{2,1,0:T(8,128)(2,1)} %all-to-all-done.1.refs_1_.refs_0_.refs_2_, bf16[32,960,128]{2,1,0:T(8,128)(2,1)} %all-to-all-done.1.refs_1_.refs_0_.refs_2_, ...), custom_call_target="tpu_custom_call", output_to_operand_aliasing={{0}: (5, {})} | custom-call | flops 6643777536 | bytes 17694720 | tf_op jit(solution)/shard_map/inverse_dft/pallas_call | solution.py:365
  652.8 12.4 %inverse_dft.6 = (bf16[3,1536,2816]{2,1,0:T(8,128)(2,1)}, f32[8,128]{1,0:T(8,128)}) custom-call(s32[1]{0:T(128)} %bitcast.count_ref, bf16[32,960,128]{2,1,0:T(8,128)(2,1)} %all-to-all-done.1.refs_1_.refs_0_.refs_2_, bf16[32,960,128]{2,1,0:T(8,128)(2,1)} %all-to-all-done.1.refs_1_.refs_0_.refs_2_, ...), custom_call_target="tpu_custom_call", output_to_operand_aliasing={{0}: (5, {})} | custom-call | flops 4429185024 | bytes 13238272 | tf_op jit(solution)/shard_map/inverse_dft/pallas_call | solution.py:365
  665.2 9.4 %all-to-all-done.5.refs_0_.refs_1_.refs_2_ = bf16[32,192,128]{2,1,0:T(8,128)(2,1)} async-done(((bf16[32,192,128]{2,1,0:T(8,128)(2,1)}), bf16[32,192,128]{2,1,0:T(8,128)(2,1)}, u32[]{:S(2)}, u32[]{:S(2)}) %all-to-all-start.5) | async-done | bytes 1572896 | tf_op jit(solution)/shard_map/all_to_all | solution.py:608
  674.5 8.7 %inverse_dft.7 = (bf16[3,1536,2816]{2,1,0:T(8,128)(2,1)}, f32[8,128]{1,0:T(8,128)}) custom-call(s32[1]{0:T(128)} %bitcast.count_ref, bf16[32,192,128]{2,1,0:T(8,128)(2,1)} %all-to-all-done.5.refs_0_.refs_1_.refs_2_, bf16[32,192,128]{2,1,0:T(8,128)(2,1)} %all-to-all-done.5.refs_0_.refs_1_.refs_2_, ...), custom_call_target="tpu_custom_call", output_to_operand_aliasing={{0}: (5, {})} | custom-call | flops 2214592512 | bytes 8781824 | tf_op jit(solution)/shard_map/inverse_dft/pallas_call | solution.py:365
  (10 shorter events, 3.1 us)
Async XLA Ops:
  11.7 45.2 %all-to-all-start.3 = ((bf16[32,1,192,128]{3,2,1,0:T(8,128)(2,1)}), bf16[32,1,192,128]{3,2,1,0:T(8,128)(2,1)}, u32[]{:S(2)}, u32[]{:S(2)}) async-start(bf16[32,1,192,128]{3,2,1,0:T(8,128)(2,1)} %forward_first.1), calls=%async_computation.3 | async-start | bytes 3145728 | tf_op jit(solution)/shard_map/all_to_all | solution.py:608
  56.8 75.3 %all-to-all-start.2 = ((bf16[32,2,192,128]{3,2,1,0:T(8,128)(2,1)}), bf16[32,2,192,128]{3,2,1,0:T(8,128)(2,1)}, u32[]{:S(2)}, u32[]{:S(2)}) async-start(bf16[32,2,192,128]{3,2,1,0:T(8,128)(2,1)} %forward_dft.3), calls=%async_computation.2 | async-start | bytes 6291456 | tf_op jit(solution)/shard_map/all_to_all | solution.py:608
  88.8 49.0 %copy-start = (f32[1280]{0:T(1024)S(1)}, f32[1280]{0:T(1024)}, u32[]{:S(2)}) copy-start(f32[1280]{0:T(1024)} %param.11) | copy-start | bytes 15364
  132.2 213.4 %all-to-all-start = ((bf16[32,6,192,128]{3,2,1,0:T(8,128)(2,1)}), bf16[32,6,192,128]{3,2,1,0:T(8,128)(2,1)}, u32[]{:S(2)}, u32[]{:S(2)}) async-start(bf16[32,6,192,128]{3,2,1,0:T(8,128)(2,1)} %forward_dft.2), calls=%async_computation | async-start | bytes 18874368 | tf_op jit(solution)/shard_map/all_to_all | solution.py:608
  345.5 109.1 %all-to-all-start.4 = ((bf16[32,576,128]{2,1,0:T(8,128)(2,1)}), bf16[32,576,128]{2,1,0:T(8,128)(2,1)}, u32[]{:S(2)}, u32[]{:S(2)}) async-start(bf16[32,576,128]{2,1,0:T(8,128)(2,1)} %ordered_after.2), calls=%async_computation.4 | async-start | bytes 9437184 | tf_op jit(solution)/shard_map/all_to_all | solution.py:608
  454.7 3.8 copy-start.1
  454.7 178.4 %all-to-all-start.1 = ((bf16[32,960,128]{2,1,0:T(8,128)(2,1)}), bf16[32,960,128]{2,1,0:T(8,128)(2,1)}, u32[]{:S(2)}, u32[]{:S(2)}) async-start(bf16[32,960,128]{2,1,0:T(8,128)(2,1)} %get-tuple-element.19), calls=%async_computation.1 | async-start | bytes 15728640 | tf_op jit(solution)/shard_map/all_to_all | solution.py:608
  633.1 41.5 %all-to-all-start.5 = ((bf16[32,192,128]{2,1,0:T(8,128)(2,1)}), bf16[32,192,128]{2,1,0:T(8,128)(2,1)}, u32[]{:S(2)}, u32[]{:S(2)}) async-start(bf16[32,192,128]{2,1,0:T(8,128)(2,1)} %ordered_after.3), calls=%async_computation.5 | async-start | bytes 3145728 | tf_op jit(solution)/shard_map/all_to_all | solution.py:608
where the time goes:
time: 692 us; the launch traced here: 684 us
  waiting for transfers between devices  414 us (60%)
  Pallas kernels  239 us (35%)
  starting transfers between devices  26.8 us (4%)
    all_to_all x6, waiting for transfers between devices, exchange(): lax.all_to_all(blocks, ('lat', 'lev'), split_axis=0, concat_axis=0, tiled...  414 us
    pallas_call x4, Pallas kernels, legendre_step(): pl.pallas_call(functools.partial(legendre_kernel, kind, first, pair_dev,...  127 us
    pallas_call x4, Pallas kernels, inverse(): pl.pallas_call(functools.partial(inverse_kernel, levels, unit, groups, fi...  53.3 us
    pallas_call x2, Pallas kernels, forward(): pl.pallas_call(functools.partial(forward_kernel, levels, unit, some), gri...  40.5 us
    all_to_all x6, starting transfers between devices, exchange(): lax.all_to_all(blocks, ('lat', 'lev'), split_axis=0, concat_axis=0, tiled...  26.8 us
  transfers between devices with their start and end apart: 6, of which 6 were waited for; matrix products, arithmetic and copies ran while one was open for 0% of the time, Pallas kernels for 32%

commit v1 on v0

--- a/solution.py
+++ b/solution.py
@@ -299,7 +299,7 @@
     spec_refs, table_ref = refs[:groups], refs[groups]
     out_ref, token_ref, turned = refs[-3:]
     devices, rows, _ = spec_refs[0].shape
-    tile = row_tile(rows, 32)
+    tile = rows if rows <= 48 else row_tile(rows, 32)
     blocks = [(i, d) for i in range(groups) for d in range(0, devices, 2 * levels)]
     base = first_row + pl.program_id(0) * rows
     half = out_ref.shape[2] // 2
@@ -346,9 +346,7 @@
 def inverse(field, first_row, size, spec, offset, groups, table, count, partial, shape, levels, unit):
     devices = spec.shape[0]
     columns, points = 2 * table.shape[1], 2 * table.shape[2]
-    tile = row_tile(size, 64 if size % 64 == 0 and offset % 64 == 0 else 32)
-    if size <= 64:
-        tile = row_tile(size, 32)
+    tile = 64 if size % 64 == 0 and offset % 64 == 0 else row_tile(size, 48)
     rows = tile * levels
 
     def part(i):
@@ -643,23 +641,23 @@
             partial=vorticity,
         )
     vorticity = exchange(ordered_after(vorticity, others))
-    late = max(16, cap // 3 // 16 * 16)
-    if late >= cap or groups * (cap - late) % cap or (cap - late) % late:
+    late = max(16, cap // 4 // 16 * 16)
+    if late >= cap or groups * cap % (cap - late) or (cap - late) % late:
         late = 0
-    main, offset = cap - late, groups * (cap - late)
-    total = offset + groups * cap
+    main, offset = cap - late, groups * cap
+    total = offset + groups * main
     back, new_divergence = step(
         "divergence",
         0,
         groups,
         0,
         others,
-        targets=[(cap, offset, total)],
+        targets=[(cap, 0, total)],
         levels=mode_depth,
         extra=(vert_modes,),
         partial=None,
     )
-    targets = [(main, 0, total)] + ([(late, 0, groups * late)] if late else [])
+    targets = [(main, offset, total)] + ([(late, 0, groups * late)] if late else [])
     back, *rest = step(
         "temperature",
         0,
@@ -684,8 +682,8 @@
     back = exchange(back)
     if late:
         last = exchange(ordered_after(rest[0], back, token))
-    out, _ = to_grid(1, 0, cap, back, offset, partial=out)
-    out, _ = to_grid(2, 0, main, back, 0, partial=out)
+    out, _ = to_grid(1, 0, cap, back, 0, partial=out)
+    out, _ = to_grid(2, 0, main, back, offset, partial=out)
     if late:
         out, _ = to_grid(2, main, late, last, 0, partial=out)
     return out.reshape(fields, cap, levels, points)

time: 692 us -> 692 us (level)
  transfers between devices with their start and end apart: 6 -> 6, of which waited for: 6 -> 5; matrix products, arithmetic and copies ran while one was open for 0% -> 0% of each run, Pallas kernels for 32% -> 32%
where the time goes in v1:
time: 692 us; the launch traced here: 684 us
  waiting for transfers between devices  413 us (60%)
  Pallas kernels  241 us (35%)
  starting transfers between devices  26.7 us (4%)
    all_to_all x6, waiting for transfers between devices, exchange(): lax.all_to_all(blocks, ('lat', 'lev'), split_axis=0, concat_axis=0, tiled...  413 us
    pallas_call x4, Pallas kernels, legendre_step(): pl.pallas_call(functools.partial(legendre_kernel, kind, first, pair_dev,...  127 us
    pallas_call x4, Pallas kernels, inverse(): pl.pallas_call(functools.partial(inverse_kernel, levels, unit, groups, fi...  54.4 us
    pallas_call x2, Pallas kernels, forward(): pl.pallas_call(functools.partial(forward_kernel, levels, unit, some), gri...  40.5 us
    all_to_all x6, starting transfers between devices, exchange(): lax.all_to_all(blocks, ('lat', 'lev'), split_axis=0, concat_axis=0, tiled...  26.7 us
  transfers between devices with their start and end apart: 6, of which 5 were waited for; matrix products, arithmetic and copies ran while one was open for 0% of the time, Pallas kernels for 32%

profile of v1, /device:TPU:0, one launch (start us, length us, event | category | flops | bytes accessed | tf_op | source)
XLA Modules:
  0.0 684.0 jit_solution(16089209364427138250)
XLA Ops:
  0.0 11.7 %forward_first.1 = bf16[32,1,192,128]{3,2,1,0:T(8,128)(2,1)} custom-call(s32[384]{0:T(512)} %pair_ref.2, bf16[3,1536,2816]{2,1,0:T(8,128)(2,1)} %bitcast.5), custom_call_target="tpu_custom_call" | custom-call | flops 2214592512 | bytes 10223616 | tf_op jit(solution)/shard_map/forward_first/pallas_call | solution.py:273
  11.7 7.4 %all-to-all-start.3 = ((bf16[32,1,192,128]{3,2,1,0:T(8,128)(2,1)}), bf16[32,1,192,128]{3,2,1,0:T(8,128)(2,1)}, u32[]{:S(2)}, u32[]{:S(2)}) async-start(bf16[32,1,192,128]{3,2,1,0:T(8,128)(2,1)} %forward_first.1), calls=%async_computation.3 | async-start | bytes 3145728 | tf_op jit(solution)/shard_map/all_to_all | solution.py:606
  19.1 6.9 %trig_table.1.table_ref.refs_3_ = bf16[2,768,1408]{2,1,0:T(8,128)(2,1)} custom-call(s32[384]{0:T(512)} %pair_ref.2), custom_call_target="tpu_custom_call" | custom-call | flops 17301504 | bytes 4325376 | tf_op jit(solution)/shard_map/trig_table/pallas_call | solution.py:131
  26.0 12.4 %forward_dft.3 = bf16[32,2,192,128]{3,2,1,0:T(8,128)(2,1)} custom-call(bf16[3,1536,2816]{2,1,0:T(8,128)(2,1)} %bitcast.6, bf16[2,768,1408]{2,1,0:T(8,128)(2,1)} %trig_table.1.table_ref.refs_3_), custom_call_target="tpu_custom_call" | custom-call | flops 4429185024 | bytes 11796480 | tf_op jit(solution)/shard_map/forward_dft/pallas_call | solution.py:217
  38.5 18.4 %all-to-all-done.3.recv_ref = bf16[32,1,192,128]{3,2,1,0:T(8,128)(2,1)} async-done(((bf16[32,1,192,128]{3,2,1,0:T(8,128)(2,1)}), bf16[32,1,192,128]{3,2,1,0:T(8,128)(2,1)}, u32[]{:S(2)}, u32[]{:S(2)}) %all-to-all-start.3) | async-done | bytes 1572896 | tf_op jit(solution)/shard_map/all_to_all | solution.py:606
  56.8 3.9 all-to-all-start.2
  60.7 28.1 %forward_dft.2 = bf16[32,6,192,128]{3,2,1,0:T(8,128)(2,1)} custom-call(bf16[3,1536,2816]{2,1,0:T(8,128)(2,1)} %bitcast.7, bf16[2,768,1408]{2,1,0:T(8,128)(2,1)} %trig_table.1.table_ref.refs_3_), custom_call_target="tpu_custom_call" | custom-call | flops 13287555072 | bytes 26738688 | tf_op jit(solution)/shard_map/forward_dft/pallas_call | solution.py:217
  88.8 43.4 %all-to-all-done.2.recv_ref = bf16[32,2,192,128]{3,2,1,0:T(8,128)(2,1)} async-done(((bf16[32,2,192,128]{3,2,1,0:T(8,128)(2,1)}), bf16[32,2,192,128]{3,2,1,0:T(8,128)(2,1)}, u32[]{:S(2)}, u32[]{:S(2)}) %all-to-all-start.2) | async-done | bytes 3145760 | tf_op jit(solution)/shard_map/all_to_all | solution.py:606
  132.2 4.2 all-to-all-start
  136.4 1.3 dynamic_slice.3.waves_ref
  138.9 14.0 %legendre_vorticity.2.rest_2_ = bf16[32,576,128]{2,1,0:T(8,128)(2,1)} custom-call(s32[8]{0:T(128)} %counts_ref.7, s32[12]{0:T(128)} %dynamic_slice.3.waves_ref, bf16[32,1,192,128]{3,2,1,0:T(8,128)(2,1)} %all-to-all-done.3.recv_ref, bf16[12,769,1280]{2,1,0:T(8,128)(2,1)} %leg_ref.7, f32[1280,128]{1,0:T(8,128)} %broadcast_in_dim.23.rest_0_, f32[1,32]{1,0:T(1,128)} %bitcast.8), custom_call_target="tpu_custom_call" | custom-call | flops 4031774720 | bytes 11020288 | tf_op jit(solution)/shard_map/legendre_vorticity/pallas_call | solution.py:552
  152.9 24.1 %legendre_vorticity.3.refs_0_ = bf16[32,576,128]{2,1,0:T(8,128)(2,1)} custom-call(s32[8]{0:T(128)} %counts_ref.7, s32[12]{0:T(128)} %dynamic_slice.3.waves_ref, bf16[32,2,192,128]{3,2,1,0:T(8,128)(2,1)} %all-to-all-done.2.recv_ref, bf16[12,769,1280]{2,1,0:T(8,128)(2,1)} %leg_ref.7, ...), custom_call_target="tpu_custom_call", output_to_operand_aliasing={{}: (6, {})} | custom-call | flops 8063549440 | bytes 22040576 | tf_op jit(solution)/shard_map/legendre_vorticity/pallas_call | solution.py:552
  177.0 168.6 %all-to-all-done.recv_ref.refs_1_ = bf16[32,6,192,128]{3,2,1,0:T(8,128)(2,1)} async-done(((bf16[32,6,192,128]{3,2,1,0:T(8,128)(2,1)}), bf16[32,6,192,128]{3,2,1,0:T(8,128)(2,1)}, u32[]{:S(2)}, u32[]{:S(2)}) %all-to-all-start) | async-done | bytes 9437216 | tf_op jit(solution)/shard_map/all_to_all | solution.py:606
  345.5 3.8 all-to-all-start.4
  349.3 52.2 %legendre_divergence.1 = (bf16[32,1008,128]{2,1,0:T(8,128)(2,1)}, f32[12,784,128]{2,1,0:T(8,128)}) custom-call(s32[8]{0:T(128)} %counts_ref.7, s32[12]{0:T(128)} %dynamic_slice.3.waves_ref, bf16[32,6,192,128]{3,2,1,0:T(8,128)(2,1)} %all-to-all-done.recv_ref.refs_1_, bf16[12,769,1280]{2,1,0:T(8,128)(2,1)} %leg_ref.7, f32[1280,128]{1,0:T(8,128)} %broadcast_in_dim.23.rest_0_, ...), custom_call_target="tpu_custom_call" | custom-call | flops 12095324160 | bytes 33060864 | tf_op jit(solution)/shard_map/legendre_divergence/pallas_call | solution.py:552
  401.5 36.8 %legendre_temperature.1 = (bf16[32,1008,128]{2,1,0:T(8,128)(2,1)}, bf16[32,144,128]{2,1,0:T(8,128)(2,1)}) custom-call(s32[8]{0:T(128)} %counts_ref.7, s32[12]{0:T(128)} %dynamic_slice.3.waves_ref, bf16[32,6,192,128]{3,2,1,0:T(8,128)(2,1)} %all-to-all-done.recv_ref.refs_1_, bf16[12,769,1280]{2,1,0:T(8,128)(2,1)} %leg_ref.7, ...), custom_call_target="tpu_custom_call", output_to_operand_aliasing={{0}: (8, {})} | custom-call | flops 12095324160 | bytes 33060864 | tf_op jit(solution)/shard_map/legendre_temperature/pallas_call | solution.py:552
  438.3 16.4 %all-to-all-done.4.refs_0_.refs_1_.refs_2_ = bf16[32,576,128]{2,1,0:T(8,128)(2,1)} async-done(((bf16[32,576,128]{2,1,0:T(8,128)(2,1)}), bf16[32,576,128]{2,1,0:T(8,128)(2,1)}, u32[]{:S(2)}, u32[]{:S(2)}) %all-to-all-start.4) | async-done | bytes 4718624 | tf_op jit(solution)/shard_map/all_to_all | solution.py:606
  454.7 3.8 all-to-all-start.1
  459.2 16.1 %inverse_dft.4 = (bf16[3,1536,2816]{2,1,0:T(8,128)(2,1)}, f32[8,128]{1,0:T(8,128)}) custom-call(s32[1]{0:T(128)} %bitcast.count_ref, bf16[32,576,128]{2,1,0:T(8,128)(2,1)} %all-to-all-done.4.refs_0_.refs_1_.refs_2_, bf16[32,576,128]{2,1,0:T(8,128)(2,1)} %all-to-all-done.4.refs_0_.refs_1_.refs_2_, ...), custom_call_target="tpu_custom_call" | custom-call | flops 6643777536 | bytes 17694720 | tf_op jit(solution)/shard_map/inverse_dft/pallas_call | solution.py:363
  475.3 166.4 %all-to-all-done.1.refs_1_.refs_0_.refs_2_ = bf16[32,1008,128]{2,1,0:T(8,128)(2,1)} async-done(((bf16[32,1008,128]{2,1,0:T(8,128)(2,1)}), bf16[32,1008,128]{2,1,0:T(8,128)(2,1)}, u32[]{:S(2)}, u32[]{:S(2)}) %all-to-all-start.1) | async-done | bytes 8257568 | tf_op jit(solution)/shard_map/all_to_all | solution.py:606
  641.7 3.6 all-to-all-start.5
  645.3 16.1 %inverse_dft.5 = (bf16[3,1536,2816]{2,1,0:T(8,128)(2,1)}, f32[8,128]{1,0:T(8,128)}) custom-call(s32[1]{0:T(128)} %bitcast.count_ref, bf16[32,1008,128]{2,1,0:T(8,128)(2,1)} %all-to-all-done.1.refs_1_.refs_0_.refs_2_, bf16[32,1008,128]{2,1,0:T(8,128)(2,1)} %all-to-all-done.1.refs_1_.refs_0_.refs_2_, ...), custom_call_target="tpu_custom_call", output_to_operand_aliasing={{0}: (5, {})} | custom-call | flops 6643777536 | bytes 17694720 | tf_op jit(solution)/shard_map/inverse_dft/pallas_call | solution.py:363
  661.4 14.4 %inverse_dft.6 = (bf16[3,1536,2816]{2,1,0:T(8,128)(2,1)}, f32[8,128]{1,0:T(8,128)}) custom-call(s32[1]{0:T(128)} %bitcast.count_ref, bf16[32,1008,128]{2,1,0:T(8,128)(2,1)} %all-to-all-done.1.refs_1_.refs_0_.refs_2_, bf16[32,1008,128]{2,1,0:T(8,128)(2,1)} %all-to-all-done.1.refs_1_.refs_0_.refs_2_, ...), custom_call_target="tpu_custom_call", output_to_operand_aliasing={{0}: (5, {})} | custom-call | flops 4982833152 | bytes 14352384 | tf_op jit(solution)/shard_map/inverse_dft/pallas_call | solution.py:363
  675.8 7.8 %inverse_dft.7 = (bf16[3,1536,2816]{2,1,0:T(8,128)(2,1)}, f32[8,128]{1,0:T(8,128)}) custom-call(s32[1]{0:T(128)} %bitcast.count_ref, bf16[32,144,128]{2,1,0:T(8,128)(2,1)} %all-to-all-done.5.refs_0_.refs_1_.refs_2_, bf16[32,144,128]{2,1,0:T(8,128)(2,1)} %all-to-all-done.5.refs_0_.refs_1_.refs_2_, ...), custom_call_target="tpu_custom_call", output_to_operand_aliasing={{0}: (5, {})} | custom-call | flops 1660944384 | bytes 7667712 | tf_op jit(solution)/shard_map/inverse_dft/pallas_call | solution.py:363
  (10 shorter events, 1.8 us)
Async XLA Ops:
  11.7 45.2 %all-to-all-start.3 = ((bf16[32,1,192,128]{3,2,1,0:T(8,128)(2,1)}), bf16[32,1,192,128]{3,2,1,0:T(8,128)(2,1)}, u32[]{:S(2)}, u32[]{:S(2)}) async-start(bf16[32,1,192,128]{3,2,1,0:T(8,128)(2,1)} %forward_first.1), calls=%async_computation.3 | async-start | bytes 3145728 | tf_op jit(solution)/shard_map/all_to_all | solution.py:606
  56.8 75.3 %all-to-all-start.2 = ((bf16[32,2,192,128]{3,2,1,0:T(8,128)(2,1)}), bf16[32,2,192,128]{3,2,1,0:T(8,128)(2,1)}, u32[]{:S(2)}, u32[]{:S(2)}) async-start(bf16[32,2,192,128]{3,2,1,0:T(8,128)(2,1)} %forward_dft.3), calls=%async_computation.2 | async-start | bytes 6291456 | tf_op jit(solution)/shard_map/all_to_all | solution.py:606
  88.8 49.0 %copy-start = (f32[1280]{0:T(1024)S(1)}, f32[1280]{0:T(1024)}, u32[]{:S(2)}) copy-start(f32[1280]{0:T(1024)} %param.11) | copy-start | bytes 15364
  132.2 213.4 %all-to-all-start = ((bf16[32,6,192,128]{3,2,1,0:T(8,128)(2,1)}), bf16[32,6,192,128]{3,2,1,0:T(8,128)(2,1)}, u32[]{:S(2)}, u32[]{:S(2)}) async-start(bf16[32,6,192,128]{3,2,1,0:T(8,128)(2,1)} %forward_dft.2), calls=%async_computation | async-start | bytes 18874368 | tf_op jit(solution)/shard_map/all_to_all | solution.py:606
  345.5 109.1 %all-to-all-start.4 = ((bf16[32,576,128]{2,1,0:T(8,128)(2,1)}), bf16[32,576,128]{2,1,0:T(8,128)(2,1)}, u32[]{:S(2)}, u32[]{:S(2)}) async-start(bf16[32,576,128]{2,1,0:T(8,128)(2,1)} %ordered_after.2), calls=%async_computation.4 | async-start | bytes 9437184 | tf_op jit(solution)/shard_map/all_to_all | solution.py:606
  454.7 3.8 copy-start.1
  454.7 187.0 %all-to-all-start.1 = ((bf16[32,1008,128]{2,1,0:T(8,128)(2,1)}), bf16[32,1008,128]{2,1,0:T(8,128)(2,1)}, u32[]{:S(2)}, u32[]{:S(2)}) async-start(bf16[32,1008,128]{2,1,0:T(8,128)(2,1)} %get-tuple-element.19), calls=%async_computation.1 | async-start | bytes 16515072 | tf_op jit(solution)/shard_map/all_to_all | solution.py:606
  641.7 34.1 %all-to-all-start.5 = ((bf16[32,144,128]{2,1,0:T(8,128)(2,1)}), bf16[32,144,128]{2,1,0:T(8,128)(2,1)}, u32[]{:S(2)}, u32[]{:S(2)}) async-start(bf16[32,144,128]{2,1,0:T(8,128)(2,1)} %ordered_after.3), calls=%async_computation.5 | async-start | bytes 2359296 | tf_op jit(solution)/shard_map/all_to_all | solution.py:606

commit v2 on v0

--- a/solution.py
+++ b/solution.py
@@ -244,43 +244,46 @@
     def _():
         fill_table(table, pair_ref, pair_dev, group, width, grid_ref.shape[2], 0, 0)
 
-    tile = grid_ref.shape[1] // levels
-    half = scratch.shape[2] * LANES
-    folded = fold(grid_ref[0])
-    for n in range(table.shape[1] // half):
-
-        def store(d, block, n=n):
-            out_ref[n * 2 * half // unit + d, 0] = block
-
-        rows = slice(n * half, (n + 1) * half)
-        emit_blocks(
-            folded,
-            [table[0, rows, :], table[1, rows, :]],
-            scratch.at[n],
-            store,
-            tile,
-            levels,
-            unit,
-        )
+    parts, half = scratch.shape[1], scratch.shape[3] * LANES
+    tile = grid_ref.shape[1] // levels // parts
+    for s in range(parts):
+        folded = fold(grid_ref[0, s * tile * levels : (s + 1) * tile * levels, :])
+        for n in range(table.shape[1] // half):
+
+            def store(d, block, s=s, n=n):
+                out_ref[n * 2 * half // unit + d, 0, s * tile : (s + 1) * tile, :] = block
+
+            rows = slice(n * half, (n + 1) * half)
+            emit_blocks(
+                folded,
+                [table[0, rows, :], table[1, rows, :]],
+                scratch.at[n, s],
+                store,
+                tile,
+                levels,
+                unit,
+            )
 
 
 def forward_first(grid, pair_m, levels, unit, devices, group, width):
     _, rows, points = grid.shape
     cap = rows // levels
     tile = row_tile(cap, 32)
+    parts = 2 if cap % (2 * tile) == 0 else 1
     columns = devices * unit
     half = devices_at_once(devices) * unit // 2
     return pl.pallas_call(
         functools.partial(first_kernel, levels, unit, pair_m.shape[0] // devices, group, width),
         grid_spec=pltpu.PrefetchScalarGridSpec(
             num_scalar_prefetch=1,
-            grid=(cap // tile,),
-            in_specs=[pl.BlockSpec((1, tile * levels, points), lambda t, m: (0, t, 0))],
-            out_specs=pl.BlockSpec((devices, 1, tile, LANES), lambda t, m: (0, 0, t, 0)),
+            grid=(cap // (parts * tile),),
+            in_specs=[pl.BlockSpec((1, parts * tile * levels, points), lambda t, m: (0, t, 0))],
+            out_specs=pl.BlockSpec((devices, 1, parts * tile, LANES), lambda t, m: (0, 0, t, 0)),
             scratch_shapes=[
                 pltpu.VMEM((2, columns // 2, points // 2), jnp.bfloat16),
                 pltpu.VMEM(
-                    (columns // 2 // half, 2, half // LANES, tile * levels, LANES), jnp.float32
+                    (columns // 2 // half, parts, 2, half // LANES, tile * levels, LANES),
+                    jnp.float32,
                 ),
             ],
         ),

time: 692 us -> 690 us (level)
  no operation moved by 1% of the time
where the time goes in v2:
time: 690 us; the launch traced here: 682 us
  waiting for transfers between devices  414 us (60%)
  Pallas kernels  238 us (34%)
  starting transfers between devices  26.8 us (4%)
    all_to_all x6, waiting for transfers between devices, exchange(): lax.all_to_all(blocks, ('lat', 'lev'), split_axis=0, concat_axis=0, tiled...  414 us
    pallas_call x4, Pallas kernels, legendre_step(): pl.pallas_call(functools.partial(legendre_kernel, kind, first, pair_dev,...  127 us
    pallas_call x4, Pallas kernels, inverse(): pl.pallas_call(functools.partial(inverse_kernel, levels, unit, groups, fi...  53.3 us
    pallas_call x2, Pallas kernels, forward(): pl.pallas_call(functools.partial(forward_kernel, levels, unit, some), gri...  40.5 us
    all_to_all x6, starting transfers between devices, exchange(): lax.all_to_all(blocks, ('lat', 'lev'), split_axis=0, concat_axis=0, tiled...  26.8 us
  transfers between devices with their start and end apart: 6, of which 6 were waited for; matrix products, arithmetic and copies ran while one was open for 0% of the time, Pallas kernels for 32%

profile of v2, /device:TPU:0, one launch (start us, length us, event | category | flops | bytes accessed | tf_op | source)
XLA Modules:
  0.0 682.0 jit_solution(8900259964545139642)
XLA Ops:
  0.0 9.9 %forward_first.1 = bf16[32,1,192,128]{3,2,1,0:T(8,128)(2,1)} custom-call(s32[384]{0:T(512)} %pair_ref.2, bf16[3,1536,2816]{2,1,0:T(8,128)(2,1)} %bitcast.5), custom_call_target="tpu_custom_call" | custom-call | flops 2214592512 | bytes 10223616 | tf_op jit(solution)/shard_map/forward_first/pallas_call | solution.py:275
  9.9 7.4 %all-to-all-start.3 = ((bf16[32,1,192,128]{3,2,1,0:T(8,128)(2,1)}), bf16[32,1,192,128]{3,2,1,0:T(8,128)(2,1)}, u32[]{:S(2)}, u32[]{:S(2)}) async-start(bf16[32,1,192,128]{3,2,1,0:T(8,128)(2,1)} %forward_first.1), calls=%async_computation.3 | async-start | bytes 3145728 | tf_op jit(solution)/shard_map/all_to_all | solution.py:611
  17.4 6.9 %trig_table.1.table_ref.refs_3_ = bf16[2,768,1408]{2,1,0:T(8,128)(2,1)} custom-call(s32[384]{0:T(512)} %pair_ref.2), custom_call_target="tpu_custom_call" | custom-call | flops 17301504 | bytes 4325376 | tf_op jit(solution)/shard_map/trig_table/pallas_call | solution.py:131
  24.3 12.5 %forward_dft.3 = bf16[32,2,192,128]{3,2,1,0:T(8,128)(2,1)} custom-call(bf16[3,1536,2816]{2,1,0:T(8,128)(2,1)} %bitcast.6, bf16[2,768,1408]{2,1,0:T(8,128)(2,1)} %trig_table.1.table_ref.refs_3_), custom_call_target="tpu_custom_call" | custom-call | flops 4429185024 | bytes 11796480 | tf_op jit(solution)/shard_map/forward_dft/pallas_call | solution.py:217
  36.8 18.3 %all-to-all-done.3.recv_ref = bf16[32,1,192,128]{3,2,1,0:T(8,128)(2,1)} async-done(((bf16[32,1,192,128]{3,2,1,0:T(8,128)(2,1)}), bf16[32,1,192,128]{3,2,1,0:T(8,128)(2,1)}, u32[]{:S(2)}, u32[]{:S(2)}) %all-to-all-start.3) | async-done | bytes 1572896 | tf_op jit(solution)/shard_map/all_to_all | solution.py:611
  55.1 3.9 all-to-all-start.2
  59.0 28.1 %forward_dft.2 = bf16[32,6,192,128]{3,2,1,0:T(8,128)(2,1)} custom-call(bf16[3,1536,2816]{2,1,0:T(8,128)(2,1)} %bitcast.7, bf16[2,768,1408]{2,1,0:T(8,128)(2,1)} %trig_table.1.table_ref.refs_3_), custom_call_target="tpu_custom_call" | custom-call | flops 13287555072 | bytes 26738688 | tf_op jit(solution)/shard_map/forward_dft/pallas_call | solution.py:217
  87.1 43.4 %all-to-all-done.2.recv_ref = bf16[32,2,192,128]{3,2,1,0:T(8,128)(2,1)} async-done(((bf16[32,2,192,128]{3,2,1,0:T(8,128)(2,1)}), bf16[32,2,192,128]{3,2,1,0:T(8,128)(2,1)}, u32[]{:S(2)}, u32[]{:S(2)}) %all-to-all-start.2) | async-done | bytes 3145760 | tf_op jit(solution)/shard_map/all_to_all | solution.py:611
  130.4 4.2 all-to-all-start
  137.1 14.0 %legendre_vorticity.2.rest_2_ = bf16[32,576,128]{2,1,0:T(8,128)(2,1)} custom-call(s32[8]{0:T(128)} %counts_ref.7, s32[12]{0:T(128)} %dynamic_slice.3.waves_ref, bf16[32,1,192,128]{3,2,1,0:T(8,128)(2,1)} %all-to-all-done.3.recv_ref, bf16[12,769,1280]{2,1,0:T(8,128)(2,1)} %leg_ref.7, f32[1280,128]{1,0:T(8,128)} %broadcast_in_dim.23.rest_0_, f32[1,32]{1,0:T(1,128)} %bitcast.8), custom_call_target="tpu_custom_call" | custom-call | flops 4031774720 | bytes 11020288 | tf_op jit(solution)/shard_map/legendre_vorticity/pallas_call | solution.py:557
  151.1 24.2 %legendre_vorticity.3.refs_0_ = bf16[32,576,128]{2,1,0:T(8,128)(2,1)} custom-call(s32[8]{0:T(128)} %counts_ref.7, s32[12]{0:T(128)} %dynamic_slice.3.waves_ref, bf16[32,2,192,128]{3,2,1,0:T(8,128)(2,1)} %all-to-all-done.2.recv_ref, bf16[12,769,1280]{2,1,0:T(8,128)(2,1)} %leg_ref.7, ...), custom_call_target="tpu_custom_call", output_to_operand_aliasing={{}: (6, {})} | custom-call | flops 8063549440 | bytes 22040576 | tf_op jit(solution)/shard_map/legendre_vorticity/pallas_call | solution.py:557
  175.3 168.5 %all-to-all-done.recv_ref.refs_1_ = bf16[32,6,192,128]{3,2,1,0:T(8,128)(2,1)} async-done(((bf16[32,6,192,128]{3,2,1,0:T(8,128)(2,1)}), bf16[32,6,192,128]{3,2,1,0:T(8,128)(2,1)}, u32[]{:S(2)}, u32[]{:S(2)}) %all-to-all-start) | async-done | bytes 9437216 | tf_op jit(solution)/shard_map/all_to_all | solution.py:611
  343.8 3.8 all-to-all-start.4
  347.6 52.2 %legendre_divergence.1 = (bf16[32,960,128]{2,1,0:T(8,128)(2,1)}, f32[12,784,128]{2,1,0:T(8,128)}) custom-call(s32[8]{0:T(128)} %counts_ref.7, s32[12]{0:T(128)} %dynamic_slice.3.waves_ref, bf16[32,6,192,128]{3,2,1,0:T(8,128)(2,1)} %all-to-all-done.recv_ref.refs_1_, bf16[12,769,1280]{2,1,0:T(8,128)(2,1)} %leg_ref.7, f32[1280,128]{1,0:T(8,128)} %broadcast_in_dim.23.rest_0_, ...), custom_call_target="tpu_custom_call" | custom-call | flops 12095324160 | bytes 33060864 | tf_op jit(solution)/shard_map/legendre_divergence/pallas_call | solution.py:557
  399.8 36.7 %legendre_temperature.1 = (bf16[32,960,128]{2,1,0:T(8,128)(2,1)}, bf16[32,192,128]{2,1,0:T(8,128)(2,1)}) custom-call(s32[8]{0:T(128)} %counts_ref.7, s32[12]{0:T(128)} %dynamic_slice.3.waves_ref, bf16[32,6,192,128]{3,2,1,0:T(8,128)(2,1)} %all-to-all-done.recv_ref.refs_1_, bf16[12,769,1280]{2,1,0:T(8,128)(2,1)} %leg_ref.7, ...), custom_call_target="tpu_custom_call", output_to_operand_aliasing={{0}: (8, {})} | custom-call | flops 12095324160 | bytes 33060864 | tf_op jit(solution)/shard_map/legendre_temperature/pallas_call | solution.py:557
  436.5 16.5 %all-to-all-done.4.refs_0_.refs_1_.refs_2_ = bf16[32,576,128]{2,1,0:T(8,128)(2,1)} async-done(((bf16[32,576,128]{2,1,0:T(8,128)(2,1)}), bf16[32,576,128]{2,1,0:T(8,128)(2,1)}, u32[]{:S(2)}, u32[]{:S(2)}) %all-to-all-start.4) | async-done | bytes 4718624 | tf_op jit(solution)/shard_map/all_to_all | solution.py:611
  452.9 3.8 all-to-all-start.1
  457.4 16.1 %inverse_dft.4 = (bf16[3,1536,2816]{2,1,0:T(8,128)(2,1)}, f32[8,128]{1,0:T(8,128)}) custom-call(s32[1]{0:T(128)} %bitcast.count_ref, bf16[32,576,128]{2,1,0:T(8,128)(2,1)} %all-to-all-done.4.refs_0_.refs_1_.refs_2_, bf16[32,576,128]{2,1,0:T(8,128)(2,1)} %all-to-all-done.4.refs_0_.refs_1_.refs_2_, ...), custom_call_target="tpu_custom_call" | custom-call | flops 6643777536 | bytes 17694720 | tf_op jit(solution)/shard_map/inverse_dft/pallas_call | solution.py:368
  473.5 157.8 %all-to-all-done.1.refs_1_.refs_0_.refs_2_ = bf16[32,960,128]{2,1,0:T(8,128)(2,1)} async-done(((bf16[32,960,128]{2,1,0:T(8,128)(2,1)}), bf16[32,960,128]{2,1,0:T(8,128)(2,1)}, u32[]{:S(2)}, u32[]{:S(2)}) %all-to-all-start.1) | async-done | bytes 7864352 | tf_op jit(solution)/shard_map/all_to_all | solution.py:611
  631.3 3.7 all-to-all-start.5
  635.0 16.1 %inverse_dft.5 = (bf16[3,1536,2816]{2,1,0:T(8,128)(2,1)}, f32[8,128]{1,0:T(8,128)}) custom-call(s32[1]{0:T(128)} %bitcast.count_ref, bf16[32,960,128]{2,1,0:T(8,128)(2,1)} %all-to-all-done.1.refs_1_.refs_0_.refs_2_, bf16[32,960,128]{2,1,0:T(8,128)(2,1)} %all-to-all-done.1.refs_1_.refs_0_.refs_2_, ...), custom_call_target="tpu_custom_call", output_to_operand_aliasing={{0}: (5, {})} | custom-call | flops 6643777536 | bytes 17694720 | tf_op jit(solution)/shard_map/inverse_dft/pallas_call | solution.py:368
  651.1 12.4 %inverse_dft.6 = (bf16[3,1536,2816]{2,1,0:T(8,128)(2,1)}, f32[8,128]{1,0:T(8,128)}) custom-call(s32[1]{0:T(128)} %bitcast.count_ref, bf16[32,960,128]{2,1,0:T(8,128)(2,1)} %all-to-all-done.1.refs_1_.refs_0_.refs_2_, bf16[32,960,128]{2,1,0:T(8,128)(2,1)} %all-to-all-done.1.refs_1_.refs_0_.refs_2_, ...), custom_call_target="tpu_custom_call", output_to_operand_aliasing={{0}: (5, {})} | custom-call | flops 4429185024 | bytes 13238272 | tf_op jit(solution)/shard_map/inverse_dft/pallas_call | solution.py:368
  663.5 9.4 %all-to-all-done.5.refs_0_.refs_1_.refs_2_ = bf16[32,192,128]{2,1,0:T(8,128)(2,1)} async-done(((bf16[32,192,128]{2,1,0:T(8,128)(2,1)}), bf16[32,192,128]{2,1,0:T(8,128)(2,1)}, u32[]{:S(2)}, u32[]{:S(2)}) %all-to-all-start.5) | async-done | bytes 1572896 | tf_op jit(solution)/shard_map/all_to_all | solution.py:611
  672.8 8.7 %inverse_dft.7 = (bf16[3,1536,2816]{2,1,0:T(8,128)(2,1)}, f32[8,128]{1,0:T(8,128)}) custom-call(s32[1]{0:T(128)} %bitcast.count_ref, bf16[32,192,128]{2,1,0:T(8,128)(2,1)} %all-to-all-done.5.refs_0_.refs_1_.refs_2_, bf16[32,192,128]{2,1,0:T(8,128)(2,1)} %all-to-all-done.5.refs_0_.refs_1_.refs_2_, ...), custom_call_target="tpu_custom_call", output_to_operand_aliasing={{0}: (5, {})} | custom-call | flops 2214592512 | bytes 8781824 | tf_op jit(solution)/shard_map/inverse_dft/pallas_call | solution.py:368
  (10 shorter events, 3.1 us)
Async XLA Ops:
  9.9 45.1 %all-to-all-start.3 = ((bf16[32,1,192,128]{3,2,1,0:T(8,128)(2,1)}), bf16[32,1,192,128]{3,2,1,0:T(8,128)(2,1)}, u32[]{:S(2)}, u32[]{:S(2)}) async-start(bf16[32,1,192,128]{3,2,1,0:T(8,128)(2,1)} %forward_first.1), calls=%async_computation.3 | async-start | bytes 3145728 | tf_op jit(solution)/shard_map/all_to_all | solution.py:611
  55.1 75.3 %all-to-all-start.2 = ((bf16[32,2,192,128]{3,2,1,0:T(8,128)(2,1)}), bf16[32,2,192,128]{3,2,1,0:T(8,128)(2,1)}, u32[]{:S(2)}, u32[]{:S(2)}) async-start(bf16[32,2,192,128]{3,2,1,0:T(8,128)(2,1)} %forward_dft.3), calls=%async_computation.2 | async-start | bytes 6291456 | tf_op jit(solution)/shard_map/all_to_all | solution.py:611
  87.1 49.0 %copy-start = (f32[1280]{0:T(1024)S(1)}, f32[1280]{0:T(1024)}, u32[]{:S(2)}) copy-start(f32[1280]{0:T(1024)} %param.11) | copy-start | bytes 15364
  130.4 213.4 %all-to-all-start = ((bf16[32,6,192,128]{3,2,1,0:T(8,128)(2,1)}), bf16[32,6,192,128]{3,2,1,0:T(8,128)(2,1)}, u32[]{:S(2)}, u32[]{:S(2)}) async-start(bf16[32,6,192,128]{3,2,1,0:T(8,128)(2,1)} %forward_dft.2), calls=%async_computation | async-start | bytes 18874368 | tf_op jit(solution)/shard_map/all_to_all | solution.py:611
  343.8 109.1 %all-to-all-start.4 = ((bf16[32,576,128]{2,1,0:T(8,128)(2,1)}), bf16[32,576,128]{2,1,0:T(8,128)(2,1)}, u32[]{:S(2)}, u32[]{:S(2)}) async-start(bf16[32,576,128]{2,1,0:T(8,128)(2,1)} %ordered_after.2), calls=%async_computation.4 | async-start | bytes 9437184 | tf_op jit(solution)/shard_map/all_to_all | solution.py:611
  452.9 3.8 copy-start.1
  452.9 178.4 %all-to-all-start.1 = ((bf16[32,960,128]{2,1,0:T(8,128)(2,1)}), bf16[32,960,128]{2,1,0:T(8,128)(2,1)}, u32[]{:S(2)}, u32[]{:S(2)}) async-start(bf16[32,960,128]{2,1,0:T(8,128)(2,1)} %get-tuple-element.19), calls=%async_computation.1 | async-start | bytes 15728640 | tf_op jit(solution)/shard_map/all_to_all | solution.py:611
  631.3 41.5 %all-to-all-start.5 = ((bf16[32,192,128]{2,1,0:T(8,128)(2,1)}), bf16[32,192,128]{2,1,0:T(8,128)(2,1)}, u32[]{:S(2)}, u32[]{:S(2)}) async-start(bf16[32,192,128]{2,1,0:T(8,128)(2,1)} %ordered_after.3), calls=%async_computation.5 | async-start | bytes 3145728 | tf_op jit(solution)/shard_map/all_to_all | solution.py:611
